TPU v7x, 256 devices: a whole 4x4x8 slice. The times are simulated.
256 devices in a mesh: wide: 64 (over x, z_lo, y, core), narrow: 4 (over z_hi).
Axes of the slice: x: 4, y: 4, z: 8 (z_hi: 4, z_lo: 2; z = z_hi * 2 + z_lo), core: 2. Of those that a mesh axis runs over, the one named last changes fastest.
Arguments:
- source_features: bfloat16 [64, 128, 1024], P('wide'), may hold values from -6 to 6
- target_features: bfloat16 [32, 128, 1024], P('narrow', 'wide'), may hold values from -6 to 6
- target_in_taps: float32 [16, 9], replicated, may hold values from -2 to 2
- target_in_bias: float32 [16], replicated, may hold values from -3 to 3
- target_out_taps: float32 [16, 9], replicated, may hold values from -1 to 1
- source_in_taps: float32 [16, 9], replicated, may hold values from -2 to 2
- source_in_bias: float32 [16], replicated, may hold values from -3 to 3
- source_out_taps: float32 [16, 9], replicated, may hold values from -1 to 1
Outputs:
- consensus: bfloat16 [32, 128, 64, 128], P('narrow', 'wide')
All inputs are finite; a program needn't handle non-finite values.
Results may differ from a plain program's by a relative error of at most 0.0072.
Values may be sent and summed in bfloat16 or wider, within the bound.
A program may use at most 192 MiB of HBM per device.

v0:
```python
import jax
import jax.numpy as jnp
from jax import lax
from jax.sharding import PartitionSpec as P


def padded_2(block, sides, width):
    for axis, dim in sides:
        count = lax.axis_size(axis)
        forward = [(i, i + 1) for i in range(count - 1)]
        backward = [(target, source) for source, target in forward]
        low = lax.ppermute(
            lax.slice_in_dim(block, block.shape[dim] - width, None, axis=dim), axis, forward
        )
        high = lax.ppermute(lax.slice_in_dim(block, 0, width, axis=dim), axis, backward)
        block = jnp.concatenate([low, block, high], axis=dim)
    return block


def conv_valid(field, weights, first_axis, second_axis):
    size_one = field.shape[first_axis] - 2
    size_two = field.shape[second_axis] - 2
    total = None
    for a in range(3):
        rows = lax.slice_in_dim(field, a, a + size_one, axis=first_axis)
        for b in range(3):
            term = weights[3 * a + b] * lax.slice_in_dim(rows, b, b + size_two, axis=second_axis)
            total = term if total is None else total + term
    return total


def pad_axis(field, axis):
    widths = [(0, 0)] * field.ndim
    widths[axis] = (1, 1)
    return jnp.pad(field, widths)


def consensus_section(field, in_taps, in_bias, out_taps, first_axis, second_axis):
    padded = pad_axis(pad_axis(field.astype(jnp.float32), first_axis), second_axis)
    total = None
    for h in range(in_taps.shape[0]):
        hidden = jnp.maximum(
            conv_valid(padded, in_taps[h], first_axis, second_axis) + in_bias[h], 0.0
        )
        hidden = pad_axis(pad_axis(hidden, first_axis), second_axis)
        term = conv_valid(hidden, out_taps[h], first_axis, second_axis)
        total = term if total is None else total + term
    return jnp.maximum(total, 0.0)


def on_device(
    source_features,
    target_features,
    target_in_taps,
    target_in_bias,
    target_out_taps,
    source_in_taps,
    source_in_bias,
    source_out_taps,
):
    src_rows, src_cols, channels = source_features.shape
    tgt_rows = target_features.shape[0]
    scale = channels ** (-0.5)
    flat_source = source_features.reshape(src_rows * src_cols, channels)
    piece = lax.all_gather(target_features, "wide", axis=1, tiled=True)
    count = piece.shape[1]
    product = (
        jnp.dot(
            piece.reshape(tgt_rows * count, channels),
            flat_source.T,
            preferred_element_type=jnp.float32,
        )
        * scale
    )
    correlation = product.astype(jnp.bfloat16).reshape(tgt_rows, count, src_rows, src_cols)
    hidden_count = target_in_taps.shape[0]
    extended = padded_2(correlation, (("narrow", 0),), 2)
    padded = pad_axis(extended.astype(jnp.float32), 1)
    rows_here = tgt_rows + 2
    row_start = lax.axis_index("narrow") * tgt_rows
    global_rows = row_start - 1 + jnp.arange(rows_here, dtype=jnp.int32)
    all_rows = tgt_rows * lax.axis_size("narrow")
    inside = (
        ((global_rows >= 0) & (global_rows < all_rows))
        .astype(jnp.float32)
        .reshape(rows_here, 1, 1, 1)
    )
    total = None
    for h in range(hidden_count):
        hidden = (
            jnp.maximum(conv_valid(padded, target_in_taps[h], 0, 1) + target_in_bias[h], 0.0)
            * inside
        )
        term = conv_valid(pad_axis(hidden, 1), target_out_taps[h], 0, 1)
        total = term if total is None else total + term
    target_section = jnp.maximum(total, 0.0).astype(jnp.bfloat16)
    sectioned = consensus_section(
        lax.all_to_all(target_section, "wide", split_axis=1, concat_axis=2, tiled=True),
        source_in_taps,
        source_in_bias,
        source_out_taps,
        2,
        3,
    )
    return sectioned.astype(jnp.bfloat16)


def solution(mesh):
    placed = (P("wide", None, None), P("narrow", "wide", None), P(), P(), P(), P(), P(), P())
    return jax.shard_map(
        on_device,
        mesh=mesh,
        in_specs=placed,
        out_specs=P("narrow", "wide", None, None),
        check_vma=False,
    )
```

profile of v0, /device:TPU:1, one launch (start us, length us, event | category | flops | bytes accessed | tf_op | source)
XLA Modules:
  0.0 642.1 jit_solution(14112754118471764952)
XLA Ops:
  69.0 50.2 %all-gather.2.cloned.1.call-done = bf16[8,128,1024]{2,0,1:T(8,128)(2,1)} async-done(((bf16[8,2,1024]{2,0,1:T(8,128)(2,1)}), bf16[8,128,1024]{2,0,1:T(8,128)(2,1)}) %all-gather.2.cloned.1.call-update) | async-done | bytes 2097168 | tf_op jit(solution)/shard_map/all_gather | solution.py:65
  131.0 7.3 %maximum_multiply_fusion.15 = f32[10,128,1,128]{3,0,2,1:T(8,128)S(1)} fusion(f32[10]{0:T(128)S(1)} %and_convert_fusion, f32[]{:T(128)} %bitcast.17, f32[]{:T(128)} %bitcast.16, f32[]{:T(128)} %bitcast.15, f32[]{:T(128)} %bitcast.14, f32[]{:T(128)} %bitcast.13, f32[]{:T(128)} %bitcast.12, f32[]{:T(128)} %bitcast.11, f32[]{:T(128)} %bitcast.10, f32[]{:T(128)} %bitcast.9, ...), kind=kLoop, calls=%fused_computation.119 | loop fusion | flops 3276800 | bytes 4850216 | tf_op jit(solution)/shard_map/mul | solution.py:91
  141.3 7.4 %maximum_multiply_fusion = f32[10,128,1,128]{3,0,2,1:T(8,128)S(1)} fusion(f32[]{:T(128)} %bitcast.302, f32[]{:T(128)} %bitcast.301, f32[]{:T(128)} %bitcast.300, f32[]{:T(128)} %bitcast.299, f32[]{:T(128)} %bitcast.298, f32[]{:T(128)} %bitcast.297, f32[]{:T(128)} %bitcast.296, f32[]{:T(128)} %bitcast.295, f32[]{:T(128)} %bitcast.294, f32[]{:T(128)} %bitcast.293, ...), kind=kLoop, calls=%fused_computation.104 | loop fusion | flops 3276800 | bytes 4850216 | tf_op jit(solution)/shard_map/mul | solution.py:91
  148.6 7.3 %maximum_multiply_fusion.1 = f32[10,128,1,128]{3,0,2,1:T(8,128)S(1)} fusion(f32[]{:T(128)} %bitcast.283, f32[]{:T(128)} %bitcast.282, f32[]{:T(128)} %bitcast.281, f32[]{:T(128)} %bitcast.280, f32[]{:T(128)} %bitcast.279, f32[]{:T(128)} %bitcast.278, f32[]{:T(128)} %bitcast.277, f32[]{:T(128)} %bitcast.276, f32[]{:T(128)} %bitcast.275, f32[]{:T(128)} %bitcast.274, ...), kind=kLoop, calls=%fused_computation.105 | loop fusion | flops 3276800 | bytes 4850216 | tf_op jit(solution)/shard_map/mul | solution.py:91
  163.1 8.2 %maximum_multiply_fusion.3 = f32[10,128,1,128]{3,0,2,1:T(8,128)} fusion(f32[]{:T(128)} %bitcast.245, f32[]{:T(128)} %bitcast.244, f32[]{:T(128)} %bitcast.243, f32[]{:T(128)} %bitcast.242, f32[]{:T(128)} %bitcast.241, f32[]{:T(128)} %bitcast.240, f32[]{:T(128)} %bitcast.239, f32[]{:T(128)} %bitcast.238, f32[]{:T(128)} %bitcast.237, f32[]{:T(128)} %bitcast.236, ...), kind=kLoop, calls=%fused_computation.107 | loop fusion | flops 3276800 | bytes 4850216 | tf_op jit(solution)/shard_map/mul | solution.py:91
  171.3 8.1 %maximum_multiply_fusion.4 = f32[10,128,1,128]{3,0,2,1:T(8,128)} fusion(f32[]{:T(128)} %bitcast.226, f32[]{:T(128)} %bitcast.225, f32[]{:T(128)} %bitcast.224, f32[]{:T(128)} %bitcast.223, f32[]{:T(128)} %bitcast.222, f32[]{:T(128)} %bitcast.221, f32[]{:T(128)} %bitcast.220, f32[]{:T(128)} %bitcast.219, f32[]{:T(128)} %bitcast.218, f32[]{:T(128)} %bitcast.217, ...), kind=kLoop, calls=%fused_computation.108 | loop fusion | flops 3276800 | bytes 4850216 | tf_op jit(solution)/shard_map/mul | solution.py:91
  179.4 8.1 %maximum_multiply_fusion.5 = f32[10,128,1,128]{3,0,2,1:T(8,128)} fusion(f32[]{:T(128)} %bitcast.207, f32[]{:T(128)} %bitcast.206, f32[]{:T(128)} %bitcast.205, f32[]{:T(128)} %bitcast.204, f32[]{:T(128)} %bitcast.203, f32[]{:T(128)} %bitcast.202, f32[]{:T(128)} %bitcast.201, f32[]{:T(128)} %bitcast.200, f32[]{:T(128)} %bitcast.199, f32[]{:T(128)} %bitcast.198, ...), kind=kLoop, calls=%fused_computation.109 | loop fusion | flops 3276800 | bytes 4850216 | tf_op jit(solution)/shard_map/mul | solution.py:91
  187.6 8.0 %maximum_multiply_fusion.6 = f32[10,128,1,128]{3,0,2,1:T(8,128)} fusion(f32[]{:T(128)} %bitcast.188, f32[]{:T(128)} %bitcast.187, f32[]{:T(128)} %bitcast.186, f32[]{:T(128)} %bitcast.185, f32[]{:T(128)} %bitcast.184, f32[]{:T(128)} %bitcast.183, f32[]{:T(128)} %bitcast.182, f32[]{:T(128)} %bitcast.181, f32[]{:T(128)} %bitcast.180, f32[]{:T(128)} %bitcast.179, ...), kind=kLoop, calls=%fused_computation.110 | loop fusion | flops 3276800 | bytes 4850216 | tf_op jit(solution)/shard_map/mul | solution.py:91
  195.6 7.9 %maximum_multiply_fusion.7 = f32[10,128,1,128]{3,0,2,1:T(8,128)} fusion(f32[]{:T(128)} %bitcast.169, f32[]{:T(128)} %bitcast.168, f32[]{:T(128)} %bitcast.167, f32[]{:T(128)} %bitcast.166, f32[]{:T(128)} %bitcast.165, f32[]{:T(128)} %bitcast.164, f32[]{:T(128)} %bitcast.163, f32[]{:T(128)} %bitcast.162, f32[]{:T(128)} %bitcast.161, f32[]{:T(128)} %bitcast.160, ...), kind=kLoop, calls=%fused_computation.111 | loop fusion | flops 3276800 | bytes 4850216 | tf_op jit(solution)/shard_map/mul | solution.py:91
  203.4 8.2 %maximum_multiply_fusion.8 = f32[10,128,1,128]{3,0,2,1:T(8,128)} fusion(f32[]{:T(128)} %bitcast.150, f32[]{:T(128)} %bitcast.149, f32[]{:T(128)} %bitcast.148, f32[]{:T(128)} %bitcast.147, f32[]{:T(128)} %bitcast.146, f32[]{:T(128)} %bitcast.145, f32[]{:T(128)} %bitcast.144, f32[]{:T(128)} %bitcast.143, f32[]{:T(128)} %bitcast.142, f32[]{:T(128)} %bitcast.141, ...), kind=kLoop, calls=%fused_computation.112 | loop fusion | flops 3276800 | bytes 4850216 | tf_op jit(solution)/shard_map/mul | solution.py:91
  211.6 8.3 %maximum_multiply_fusion.9 = f32[10,128,1,128]{3,0,2,1:T(8,128)} fusion(f32[]{:T(128)} %bitcast.131, f32[]{:T(128)} %bitcast.130, f32[]{:T(128)} %bitcast.129, f32[]{:T(128)} %bitcast.128, f32[]{:T(128)} %bitcast.127, f32[]{:T(128)} %bitcast.126, f32[]{:T(128)} %bitcast.125, f32[]{:T(128)} %bitcast.124, f32[]{:T(128)} %bitcast.123, f32[]{:T(128)} %bitcast.122, ...), kind=kLoop, calls=%fused_computation.113 | loop fusion | flops 3276800 | bytes 4850216 | tf_op jit(solution)/shard_map/mul | solution.py:91
  220.0 8.2 %maximum_multiply_fusion.10 = f32[10,128,1,128]{3,0,2,1:T(8,128)} fusion(f32[]{:T(128)} %bitcast.112, f32[]{:T(128)} %bitcast.111, f32[]{:T(128)} %bitcast.110, f32[]{:T(128)} %bitcast.109, f32[]{:T(128)} %bitcast.108, f32[]{:T(128)} %bitcast.107, f32[]{:T(128)} %bitcast.106, f32[]{:T(128)} %bitcast.105, f32[]{:T(128)} %bitcast.104, f32[]{:T(128)} %bitcast.103, ...), kind=kLoop, calls=%fused_computation.114 | loop fusion | flops 3276800 | bytes 4850216 | tf_op jit(solution)/shard_map/mul | solution.py:91
  228.2 8.4 %maximum_multiply_fusion.11 = f32[10,128,1,128]{3,0,2,1:T(8,128)} fusion(f32[]{:T(128)} %bitcast.93, f32[]{:T(128)} %bitcast.92, f32[]{:T(128)} %bitcast.91, f32[]{:T(128)} %bitcast.90, f32[]{:T(128)} %bitcast.89, f32[]{:T(128)} %bitcast.88, f32[]{:T(128)} %bitcast.87, f32[]{:T(128)} %bitcast.86, f32[]{:T(128)} %bitcast.85, f32[]{:T(128)} %bitcast.84, ...), kind=kLoop, calls=%fused_computation.115 | loop fusion | flops 3276800 | bytes 4850216 | tf_op jit(solution)/shard_map/mul | solution.py:91
  236.5 8.1 %maximum_multiply_fusion.12 = f32[10,128,1,128]{3,0,2,1:T(8,128)} fusion(f32[]{:T(128)} %bitcast.74, f32[]{:T(128)} %bitcast.73, f32[]{:T(128)} %bitcast.72, f32[]{:T(128)} %bitcast.71, f32[]{:T(128)} %bitcast.70, f32[]{:T(128)} %bitcast.69, f32[]{:T(128)} %bitcast.68, f32[]{:T(128)} %bitcast.67, f32[]{:T(128)} %bitcast.66, f32[]{:T(128)} %bitcast.65, ...), kind=kLoop, calls=%fused_computation.116 | loop fusion | flops 3276800 | bytes 4850216 | tf_op jit(solution)/shard_map/mul | solution.py:91
  244.6 8.4 %maximum_multiply_fusion.13 = f32[10,128,1,128]{3,0,2,1:T(8,128)} fusion(f32[]{:T(128)} %bitcast.55, f32[]{:T(128)} %bitcast.54, f32[]{:T(128)} %bitcast.53, f32[]{:T(128)} %bitcast.52, f32[]{:T(128)} %bitcast.51, f32[]{:T(128)} %bitcast.50, f32[]{:T(128)} %bitcast.49, f32[]{:T(128)} %bitcast.48, f32[]{:T(128)} %bitcast.47, f32[]{:T(128)} %bitcast.46, ...), kind=kLoop, calls=%fused_computation.117 | loop fusion | flops 3276800 | bytes 4850216 | tf_op jit(solution)/shard_map/mul | solution.py:91
  253.0 8.4 %maximum_multiply_fusion.14 = f32[10,128,1,128]{3,0,2,1:T(8,128)} fusion(f32[]{:T(128)} %bitcast.36, f32[]{:T(128)} %bitcast.35, f32[]{:T(128)} %bitcast.34, f32[]{:T(128)} %bitcast.33, f32[]{:T(128)} %bitcast.32, f32[]{:T(128)} %bitcast.31, f32[]{:T(128)} %bitcast.30, f32[]{:T(128)} %bitcast.29, f32[]{:T(128)} %bitcast.28, f32[]{:T(128)} %bitcast.27, ...), kind=kLoop, calls=%fused_computation.118 | loop fusion | flops 3276800 | bytes 4850216 | tf_op jit(solution)/shard_map/mul | solution.py:91
  261.4 133.5 %fusion.610 = bf16[8,128,1,128]{3,0,2,1:T(8,128)(2,1)} fusion(f32[10,128,1,128]{3,0,2,1:T(8,128)S(1)} %maximum_multiply_fusion, f32[]{:T(128)} %bitcast.310, f32[]{:T(128)} %bitcast.309, f32[]{:T(128)} %bitcast.308, f32[]{:T(128)} %bitcast.307, f32[]{:T(128)} %bitcast.306, f32[]{:T(128)} %bitcast.305, f32[]{:T(128)} %bitcast.304, f32[]{:T(128)} %bitcast.303, ...), kind=kLoop, calls=%fused_computation.882 | loop fusion | flops 37486592 | bytes 42277376 | tf_op jit(solution)/shard_map/convert_element_type | solution.py:96
  395.0 8.0 %all-to-all-start = ((bf16[8,128,1,128]{3,0,2,1:T(8,128)(2,1)}), bf16[8,128,1,128]{3,0,2,1:T(8,128)(2,1)S(1)}, u32[]{:S(2)}, u32[]{:S(2)}) async-start(bf16[8,128,1,128]{3,0,2,1:T(8,128)(2,1)} %fusion.610), calls=%async_computation | async-start | bytes 524288 | tf_op jit(solution)/shard_map/all_to_all | solution.py:98
  448.3 7.2 %fusion.573 = f32[8,2,64,128]{3,0,1,2:T(8,128)S(1)} fusion(bf16[8,64,2,1,128]{4,0,2,1,3:T(8,128)(2,1)S(1)} %bitcast.887, f32[]{:T(128)} %bitcast.516, f32[]{:T(128)} %bitcast.515, f32[]{:T(128)} %bitcast.514, f32[]{:T(128)} %bitcast.513, f32[]{:T(128)} %bitcast.512, f32[]{:T(128)} %bitcast.511, f32[]{:T(128)} %bitcast.510, f32[]{:T(128)} %bitcast.509, ...), kind=kLoop, calls=%fused_computation.844 | loop fusion | flops 2621440 | bytes 1851432 | tf_op jit(solution)/shard_map/max | solution.py:42
  455.5 7.2 %fusion.566 = f32[8,2,64,128]{3,0,1,2:T(8,128)S(1)} fusion(bf16[8,64,2,1,128]{4,0,2,1,3:T(8,128)(2,1)S(1)} %bitcast.888, f32[]{:T(128)} %bitcast.497, f32[]{:T(128)} %bitcast.496, f32[]{:T(128)} %bitcast.495, f32[]{:T(128)} %bitcast.494, f32[]{:T(128)} %bitcast.493, f32[]{:T(128)} %bitcast.492, f32[]{:T(128)} %bitcast.491, f32[]{:T(128)} %bitcast.490, ...), kind=kLoop, calls=%fused_computation.837 | loop fusion | flops 2621440 | bytes 1851432 | tf_op jit(solution)/shard_map/max | solution.py:42
  498.4 7.2 %fusion.524 = f32[8,2,64,128]{3,0,1,2:T(8,128)S(1)} fusion(bf16[8,64,2,1,128]{4,0,2,1,3:T(8,128)(2,1)S(1)} %bitcast.894, f32[]{:T(128)} %bitcast.383, f32[]{:T(128)} %bitcast.382, f32[]{:T(128)} %bitcast.381, f32[]{:T(128)} %bitcast.380, f32[]{:T(128)} %bitcast.379, f32[]{:T(128)} %bitcast.378, f32[]{:T(128)} %bitcast.377, f32[]{:T(128)} %bitcast.376, ...), kind=kLoop, calls=%fused_computation.795 | loop fusion | flops 2621440 | bytes 1851432 | tf_op jit(solution)/shard_map/max | solution.py:42
  512.8 7.3 %fusion.510 = f32[8,2,64,128]{3,0,1,2:T(8,128)S(1)} fusion(bf16[8,64,2,1,128]{4,0,2,1,3:T(8,128)(2,1)S(1)} %bitcast.896, f32[]{:T(128)} %bitcast.345, f32[]{:T(128)} %bitcast.344, f32[]{:T(128)} %bitcast.343, f32[]{:T(128)} %bitcast.342, f32[]{:T(128)} %bitcast.341, f32[]{:T(128)} %bitcast.339, f32[]{:T(128)} %bitcast.338, f32[]{:T(128)} %bitcast.337, ...), kind=kLoop, calls=%fused_computation.781 | loop fusion | flops 2621440 | bytes 1851432 | tf_op jit(solution)/shard_map/max | solution.py:42
  520.2 7.7 %broadcast_multiply_fusion = (f32[8,2,64,128]{3,0,1,2:T(8,128)S(1)}, f32[8,2,64,128]{3,0,1,2:T(8,128)S(1)}) fusion(f32[]{:T(128)} %bitcast.329, f32[]{:T(128)} %bitcast.325, f32[]{:T(128)} %bitcast.324, f32[]{:T(128)} %bitcast.323, f32[]{:T(128)} %bitcast.322, f32[]{:T(128)} %bitcast.321, bf16[8,64,2,1,128]{4,0,2,1,3:T(8,128)(2,1)S(1)} %bitcast.897, ...), kind=kLoop, calls=%fused_computation.884 | loop fusion | flops 2752512 | bytes 2375724 | tf_op jit(solution)/shard_map/mul | solution.py:27
  527.9 106.1 %fusion.609 = bf16[8,2,64,128]{3,0,1,2:T(8,128)(2,1)S(1)} fusion(f32[8,2,66,128]{3,0,1,2:T(8,128)S(1)} %pad.206, f32[8,2,64,128]{3,0,1,2:T(8,128)S(1)} %fusion.608, f32[]{:T(128)} %bitcast.619, f32[]{:T(128)} %bitcast.618, f32[]{:T(128)} %bitcast.617, f32[]{:T(128)} %bitcast.616, f32[]{:T(128)} %bitcast.615, f32[]{:T(128)} %bitcast.614, f32[]{:T(128)} %bitcast.613, ...), kind=kLoop, calls=%fused_computation.881 | loop fusion | flops 37748736 | bytes 34079292 | tf_op jit(solution)/shard_map/convert_element_type | solution.py:105
  (90 shorter events, 173.0 us)
Async XLA Ops:
  6.5 115.4 %copy-start = (bf16[1,128,1024]{2,1,0:T(8,128)(2,1)S(1)}, bf16[1,128,1024]{2,1,0:T(8,128)(2,1)}, u32[]{:S(2)}) copy-start(bf16[1,128,1024]{2,1,0:T(8,128)(2,1)} %param.8) | copy-start | bytes 786436
  6.5 112.7 %all-gather.2.cloned.1.call-start = ((), (), s32[]{:S(2)}) async-start(), calls=%async_computation.1 | async-start | bytes 2129920 | tf_op jit(solution)/shard_map/all_gather | solution.py:65
  122.8 7.9 %collective-permute-start.1 = (bf16[2,128,1,128]{3,0,2,1:T(2,128)(2,1)S(1)}, bf16[2,128,1,128]{3,0,2,1:T(2,128)(2,1)S(1)}, u32[]{:S(2)}, u32[]{:S(2)}) collective-permute-start(bf16[2,128,1,128]{3,0,2,1:T(2,128)(2,1)S(1)} %copy.22), channel_id=1, source_target_pairs={{1,0},{2,1},{3,2},{5,4},{6,5},{7,6},{9,8},{10,9},{11,10},{13,12},{... | collective-permute-start | bytes 196616 | tf_op jit(solution)/shard_map/ppermute | solution.py:15
  124.1 6.5 %collective-permute-start = (bf16[2,128,1,128]{3,0,2,1:T(2,128)(2,1)S(1)}, bf16[2,128,1,128]{3,0,2,1:T(2,128)(2,1)S(1)}, u32[]{:S(2)}, u32[]{:S(2)}) collective-permute-start(bf16[2,128,1,128]{3,0,2,1:T(2,128)(2,1)S(1)} %copy.21), channel_id=1, source_target_pairs={{0,1},{1,2},{2,3},{4,5},{5,6},{6,7},{8,9},{9,10},{10,11},{12,13},{... | collective-permute-start | bytes 196616 | tf_op jit(solution)/shard_map/ppermute | solution.py:12
  138.2 3.0 copy-start.1
  261.4 141.6 %copy-start.2 = (f32[16,9]{1,0:T(8,128)S(1)}, f32[16,9]{1,0:T(8,128)}, u32[]{:S(2)}) copy-start(f32[16,9]{1,0:T(8,128)} %param.15) | copy-start | bytes 1732
  261.4 142.3 %copy-start.3 = (f32[16,9]{1,0:T(8,128)S(1)}, f32[16,9]{1,0:T(8,128)}, u32[]{:S(2)}) copy-start(f32[16,9]{1,0:T(8,128)} %param.13) | copy-start | bytes 1732
  395.0 17.6 %all-to-all-start = ((bf16[8,128,1,128]{3,0,2,1:T(8,128)(2,1)}), bf16[8,128,1,128]{3,0,2,1:T(8,128)(2,1)S(1)}, u32[]{:S(2)}, u32[]{:S(2)}) async-start(bf16[8,128,1,128]{3,0,2,1:T(8,128)(2,1)} %fusion.610), calls=%async_computation | async-start | bytes 524288 | tf_op jit(solution)/shard_map/all_to_all | solution.py:98
Sparse Core Ops, SparseCore 0:
  9.2 109.9 all-gather.1
where the time goes:
time: 654 us; the launch traced here: 642 us
  other arithmetic  485 us (74%)
  local copies, waits for them, and re-layouts  70.3 us (11%)
  waiting for transfers between devices  57.2 us (9%)
  starting transfers between devices  14.7 us (2%)
  between operations  14.4 us (2%)
    convert_element_type x1, other arithmetic, on_device(): target_section = jnp.maximum(total, 0.0).astype(jnp.bfloat16)  134 us
    mul x16, other arithmetic, on_device(): jnp.maximum(conv_valid(padded, target_in_taps[h], 0, 1) + target_in_bias[...  127 us
    max x15, other arithmetic, consensus_section(): jnp.maximum(conv_valid(padded, in_taps[h], first_axis, second_axis) + in_...  107 us
    convert_element_type x1, other arithmetic, on_device(): return sectioned.astype(jnp.bfloat16)  106 us
    slice x32, local copies, waits for them, and re-layouts, conv_valid(): weights[3 * a + b]  60.5 us
    all_gather x1, waiting for transfers between devices, on_device(): piece = lax.all_gather(target_features, 'wide', axis=1, tiled=True)  50.2 us
  transfers between devices with their start and end apart: 4, of which 3 were waited for; matrix products, arithmetic and copies ran while one was open for 10% of the time, Pallas kernels for 0%

commit v1 on v0

--- a/solution.py
+++ b/solution.py
@@ -95,7 +95,12 @@
         total = term if total is None else total + term
     target_section = jnp.maximum(total, 0.0).astype(jnp.bfloat16)
     sectioned = consensus_section(
-        lax.all_to_all(target_section, "wide", split_axis=1, concat_axis=2, tiled=True),
+        jnp.concatenate(
+            lax.all_to_all(
+                jnp.stack(jnp.split(target_section, lax.axis_size("wide"), axis=1)), "wide", 0, 0
+            ),
+            axis=2,
+        ),
         source_in_taps,
         source_in_bias,
         source_out_taps,

time: 654 us -> 737 us (1.13)
  local copies, waits for them, and re-layouts: 70.3 us -> 152 us
    unnamed x9 -> x72, local copies, waits for them, and re-layouts: 1.44 us -> 81.9 us
  transfers between devices with their start and end apart: 4 -> 4, of which waited for: 3 -> 3; matrix products, arithmetic and copies ran while one was open for 10% -> 9% of each run, Pallas kernels for 0% -> 0%
where the time goes in v1:
time: 737 us; the launch traced here: 724 us
  other arithmetic  485 us (66%)
  local copies, waits for them, and re-layouts  152 us (21%)
  waiting for transfers between devices  57.2 us (8%)
  starting transfers between devices  14.7 us (2%)
  between operations  14.4 us (2%)
    convert_element_type x1, other arithmetic, on_device(): target_section = jnp.maximum(total, 0.0).astype(jnp.bfloat16)  133 us
    mul x16, other arithmetic, on_device(): jnp.maximum(conv_valid(padded, target_in_taps[h], 0, 1) + target_in_bias[...  127 us
    max x15, other arithmetic, consensus_section(): jnp.maximum(conv_valid(padded, in_taps[h], first_axis, second_axis) + in_...  107 us
    convert_element_type x1, other arithmetic, on_device(): return sectioned.astype(jnp.bfloat16)  106 us
    unnamed x72, local copies, waits for them, and re-layouts  81.9 us
    slice x32, local copies, waits for them, and re-layouts, conv_valid(): weights[3 * a + b]  60.5 us
    all_gather x1, waiting for transfers between devices, on_device(): piece = lax.all_gather(target_features, 'wide', axis=1, tiled=True)  50.2 us
  transfers between devices with their start and end apart: 4, of which 3 were waited for; matrix products, arithmetic and copies ran while one was open for 9% of the time, Pallas kernels for 0%

profile of v1, /device:TPU:1, one launch (start us, length us, event | category | flops | bytes accessed | tf_op | source)
XLA Modules:
  0.0 723.8 jit_solution(3335019208070952433)
XLA Ops:
  69.0 50.2 %all-gather.2.cloned.1.call-done = bf16[8,128,1024]{2,0,1:T(8,128)(2,1)} async-done(((bf16[8,2,1024]{2,0,1:T(8,128)(2,1)}), bf16[8,128,1024]{2,0,1:T(8,128)(2,1)}) %all-gather.2.cloned.1.call-update) | async-done | bytes 2097168 | tf_op jit(solution)/shard_map/all_gather | solution.py:65
  131.0 7.3 %maximum_multiply_fusion.15 = f32[10,128,1,128]{3,0,1,2:T(8,128)S(1)} fusion(f32[10]{0:T(128)S(1)} %and_convert_fusion, f32[]{:T(128)} %bitcast.17, f32[]{:T(128)} %bitcast.16, f32[]{:T(128)} %bitcast.15, f32[]{:T(128)} %bitcast.14, f32[]{:T(128)} %bitcast.13, f32[]{:T(128)} %bitcast.12, f32[]{:T(128)} %bitcast.11, f32[]{:T(128)} %bitcast.10, f32[]{:T(128)} %bitcast.9, ...), kind=kLoop, calls=%fused_computation.119 | loop fusion | flops 3276800 | bytes 4850216 | tf_op jit(solution)/shard_map/mul | solution.py:91
  141.3 7.4 %maximum_multiply_fusion = f32[10,128,1,128]{3,0,1,2:T(8,128)S(1)} fusion(f32[]{:T(128)} %bitcast.302, f32[]{:T(128)} %bitcast.301, f32[]{:T(128)} %bitcast.300, f32[]{:T(128)} %bitcast.299, f32[]{:T(128)} %bitcast.298, f32[]{:T(128)} %bitcast.297, f32[]{:T(128)} %bitcast.296, f32[]{:T(128)} %bitcast.295, f32[]{:T(128)} %bitcast.294, f32[]{:T(128)} %bitcast.293, ...), kind=kLoop, calls=%fused_computation.104 | loop fusion | flops 3276800 | bytes 4850216 | tf_op jit(solution)/shard_map/mul | solution.py:91
  148.7 7.3 %maximum_multiply_fusion.1 = f32[10,128,1,128]{3,0,1,2:T(8,128)S(1)} fusion(f32[]{:T(128)} %bitcast.283, f32[]{:T(128)} %bitcast.282, f32[]{:T(128)} %bitcast.281, f32[]{:T(128)} %bitcast.280, f32[]{:T(128)} %bitcast.279, f32[]{:T(128)} %bitcast.278, f32[]{:T(128)} %bitcast.277, f32[]{:T(128)} %bitcast.276, f32[]{:T(128)} %bitcast.275, f32[]{:T(128)} %bitcast.274, ...), kind=kLoop, calls=%fused_computation.105 | loop fusion | flops 3276800 | bytes 4850216 | tf_op jit(solution)/shard_map/mul | solution.py:91
  163.1 8.2 %maximum_multiply_fusion.3 = f32[10,128,1,128]{3,0,1,2:T(8,128)} fusion(f32[]{:T(128)} %bitcast.245, f32[]{:T(128)} %bitcast.244, f32[]{:T(128)} %bitcast.243, f32[]{:T(128)} %bitcast.242, f32[]{:T(128)} %bitcast.241, f32[]{:T(128)} %bitcast.240, f32[]{:T(128)} %bitcast.239, f32[]{:T(128)} %bitcast.238, f32[]{:T(128)} %bitcast.237, f32[]{:T(128)} %bitcast.236, ...), kind=kLoop, calls=%fused_computation.107 | loop fusion | flops 3276800 | bytes 4850216 | tf_op jit(solution)/shard_map/mul | solution.py:91
  171.3 8.1 %maximum_multiply_fusion.4 = f32[10,128,1,128]{3,0,1,2:T(8,128)} fusion(f32[]{:T(128)} %bitcast.226, f32[]{:T(128)} %bitcast.225, f32[]{:T(128)} %bitcast.224, f32[]{:T(128)} %bitcast.223, f32[]{:T(128)} %bitcast.222, f32[]{:T(128)} %bitcast.221, f32[]{:T(128)} %bitcast.220, f32[]{:T(128)} %bitcast.219, f32[]{:T(128)} %bitcast.218, f32[]{:T(128)} %bitcast.217, ...), kind=kLoop, calls=%fused_computation.108 | loop fusion | flops 3276800 | bytes 4850216 | tf_op jit(solution)/shard_map/mul | solution.py:91
  179.5 8.1 %maximum_multiply_fusion.5 = f32[10,128,1,128]{3,0,1,2:T(8,128)} fusion(f32[]{:T(128)} %bitcast.207, f32[]{:T(128)} %bitcast.206, f32[]{:T(128)} %bitcast.205, f32[]{:T(128)} %bitcast.204, f32[]{:T(128)} %bitcast.203, f32[]{:T(128)} %bitcast.202, f32[]{:T(128)} %bitcast.201, f32[]{:T(128)} %bitcast.200, f32[]{:T(128)} %bitcast.199, f32[]{:T(128)} %bitcast.198, ...), kind=kLoop, calls=%fused_computation.109 | loop fusion | flops 3276800 | bytes 4850216 | tf_op jit(solution)/shard_map/mul | solution.py:91
  187.6 8.0 %maximum_multiply_fusion.6 = f32[10,128,1,128]{3,0,1,2:T(8,128)} fusion(f32[]{:T(128)} %bitcast.188, f32[]{:T(128)} %bitcast.187, f32[]{:T(128)} %bitcast.186, f32[]{:T(128)} %bitcast.185, f32[]{:T(128)} %bitcast.184, f32[]{:T(128)} %bitcast.183, f32[]{:T(128)} %bitcast.182, f32[]{:T(128)} %bitcast.181, f32[]{:T(128)} %bitcast.180, f32[]{:T(128)} %bitcast.179, ...), kind=kLoop, calls=%fused_computation.110 | loop fusion | flops 3276800 | bytes 4850216 | tf_op jit(solution)/shard_map/mul | solution.py:91
  195.6 7.9 %maximum_multiply_fusion.7 = f32[10,128,1,128]{3,0,1,2:T(8,128)} fusion(f32[]{:T(128)} %bitcast.169, f32[]{:T(128)} %bitcast.168, f32[]{:T(128)} %bitcast.167, f32[]{:T(128)} %bitcast.166, f32[]{:T(128)} %bitcast.165, f32[]{:T(128)} %bitcast.164, f32[]{:T(128)} %bitcast.163, f32[]{:T(128)} %bitcast.162, f32[]{:T(128)} %bitcast.161, f32[]{:T(128)} %bitcast.160, ...), kind=kLoop, calls=%fused_computation.111 | loop fusion | flops 3276800 | bytes 4850216 | tf_op jit(solution)/shard_map/mul | solution.py:91
  203.5 8.2 %maximum_multiply_fusion.8 = f32[10,128,1,128]{3,0,1,2:T(8,128)} fusion(f32[]{:T(128)} %bitcast.150, f32[]{:T(128)} %bitcast.149, f32[]{:T(128)} %bitcast.148, f32[]{:T(128)} %bitcast.147, f32[]{:T(128)} %bitcast.146, f32[]{:T(128)} %bitcast.145, f32[]{:T(128)} %bitcast.144, f32[]{:T(128)} %bitcast.143, f32[]{:T(128)} %bitcast.142, f32[]{:T(128)} %bitcast.141, ...), kind=kLoop, calls=%fused_computation.112 | loop fusion | flops 3276800 | bytes 4850216 | tf_op jit(solution)/shard_map/mul | solution.py:91
  211.7 8.3 %maximum_multiply_fusion.9 = f32[10,128,1,128]{3,0,1,2:T(8,128)} fusion(f32[]{:T(128)} %bitcast.131, f32[]{:T(128)} %bitcast.130, f32[]{:T(128)} %bitcast.129, f32[]{:T(128)} %bitcast.128, f32[]{:T(128)} %bitcast.127, f32[]{:T(128)} %bitcast.126, f32[]{:T(128)} %bitcast.125, f32[]{:T(128)} %bitcast.124, f32[]{:T(128)} %bitcast.123, f32[]{:T(128)} %bitcast.122, ...), kind=kLoop, calls=%fused_computation.113 | loop fusion | flops 3276800 | bytes 4850216 | tf_op jit(solution)/shard_map/mul | solution.py:91
  220.0 8.2 %maximum_multiply_fusion.10 = f32[10,128,1,128]{3,0,1,2:T(8,128)} fusion(f32[]{:T(128)} %bitcast.112, f32[]{:T(128)} %bitcast.111, f32[]{:T(128)} %bitcast.110, f32[]{:T(128)} %bitcast.109, f32[]{:T(128)} %bitcast.108, f32[]{:T(128)} %bitcast.107, f32[]{:T(128)} %bitcast.106, f32[]{:T(128)} %bitcast.105, f32[]{:T(128)} %bitcast.104, f32[]{:T(128)} %bitcast.103, ...), kind=kLoop, calls=%fused_computation.114 | loop fusion | flops 3276800 | bytes 4850216 | tf_op jit(solution)/shard_map/mul | solution.py:91
  228.2 8.4 %maximum_multiply_fusion.11 = f32[10,128,1,128]{3,0,1,2:T(8,128)} fusion(f32[]{:T(128)} %bitcast.93, f32[]{:T(128)} %bitcast.92, f32[]{:T(128)} %bitcast.91, f32[]{:T(128)} %bitcast.90, f32[]{:T(128)} %bitcast.89, f32[]{:T(128)} %bitcast.88, f32[]{:T(128)} %bitcast.87, f32[]{:T(128)} %bitcast.86, f32[]{:T(128)} %bitcast.85, f32[]{:T(128)} %bitcast.84, ...), kind=kLoop, calls=%fused_computation.115 | loop fusion | flops 3276800 | bytes 4850216 | tf_op jit(solution)/shard_map/mul | solution.py:91
  236.6 8.1 %maximum_multiply_fusion.12 = f32[10,128,1,128]{3,0,1,2:T(8,128)} fusion(f32[]{:T(128)} %bitcast.74, f32[]{:T(128)} %bitcast.73, f32[]{:T(128)} %bitcast.72, f32[]{:T(128)} %bitcast.71, f32[]{:T(128)} %bitcast.70, f32[]{:T(128)} %bitcast.69, f32[]{:T(128)} %bitcast.68, f32[]{:T(128)} %bitcast.67, f32[]{:T(128)} %bitcast.66, f32[]{:T(128)} %bitcast.65, ...), kind=kLoop, calls=%fused_computation.116 | loop fusion | flops 3276800 | bytes 4850216 | tf_op jit(solution)/shard_map/mul | solution.py:91
  244.7 8.4 %maximum_multiply_fusion.13 = f32[10,128,1,128]{3,0,1,2:T(8,128)} fusion(f32[]{:T(128)} %bitcast.55, f32[]{:T(128)} %bitcast.54, f32[]{:T(128)} %bitcast.53, f32[]{:T(128)} %bitcast.52, f32[]{:T(128)} %bitcast.51, f32[]{:T(128)} %bitcast.50, f32[]{:T(128)} %bitcast.49, f32[]{:T(128)} %bitcast.48, f32[]{:T(128)} %bitcast.47, f32[]{:T(128)} %bitcast.46, ...), kind=kLoop, calls=%fused_computation.117 | loop fusion | flops 3276800 | bytes 4850216 | tf_op jit(solution)/shard_map/mul | solution.py:91
  253.0 8.3 %maximum_multiply_fusion.14 = f32[10,128,1,128]{3,0,1,2:T(8,128)} fusion(f32[]{:T(128)} %bitcast.36, f32[]{:T(128)} %bitcast.35, f32[]{:T(128)} %bitcast.34, f32[]{:T(128)} %bitcast.33, f32[]{:T(128)} %bitcast.32, f32[]{:T(128)} %bitcast.31, f32[]{:T(128)} %bitcast.30, f32[]{:T(128)} %bitcast.29, f32[]{:T(128)} %bitcast.28, f32[]{:T(128)} %bitcast.27, ...), kind=kLoop, calls=%fused_computation.118 | loop fusion | flops 3276800 | bytes 4850216 | tf_op jit(solution)/shard_map/mul | solution.py:91
  261.4 133.3 %fusion.610 = bf16[8,128,1,128]{3,0,1,2:T(8,128)(2,1)} fusion(f32[10,128,1,128]{3,0,1,2:T(8,128)S(1)} %maximum_multiply_fusion, f32[]{:T(128)} %bitcast.310, f32[]{:T(128)} %bitcast.309, f32[]{:T(128)} %bitcast.308, f32[]{:T(128)} %bitcast.307, f32[]{:T(128)} %bitcast.306, f32[]{:T(128)} %bitcast.305, f32[]{:T(128)} %bitcast.304, f32[]{:T(128)} %bitcast.303, ...), kind=kLoop, calls=%fused_computation.882 | loop fusion | flops 37486592 | bytes 42277376 | tf_op jit(solution)/shard_map/convert_element_type | solution.py:96
  476.4 8.0 %all-to-all-start = ((bf16[64,8,2,1,128]{4,1,3,2,0:T(8,128)(2,1)}), bf16[64,8,2,1,128]{4,1,3,2,0:T(8,128)(2,1)S(1)}, u32[]{:S(2)}, u32[]{:S(2)}) async-start(bf16[64,8,2,1,128]{4,1,3,2,0:T(8,128)(2,1)} %constant_dynamic-update-slice_fusion), calls=%async_computation | async-start | bytes 524288 | tf_op jit(solution)/shard_map/all_to_all | solution.py:99
  529.9 7.2 fusion.573
  551.5 7.2 fusion.552
  580.2 7.2 fusion.524
  594.7 7.3 %fusion.510 = f32[8,2,64,128]{3,0,1,2:T(8,128)S(1)} fusion(bf16[64,8,2,1,128]{4,1,3,2,0:T(8,128)(2,1)S(1)} %all-to-all-done, f32[]{:T(128)} %bitcast.467, f32[]{:T(128)} %bitcast.466, f32[]{:T(128)} %bitcast.465, f32[]{:T(128)} %bitcast.464, f32[]{:T(128)} %bitcast.463, f32[]{:T(128)} %bitcast.462, f32[]{:T(128)} %bitcast.461, f32[]{:T(128)} %bitcast.460, ...), kind=kLoop, calls=%fused_computation.781 | loop fusion | flops 2621440 | bytes 1851432 | tf_op jit(solution)/shard_map/max | solution.py:42
  602.1 7.8 %broadcast_multiply_fusion = (f32[8,2,64,128]{3,0,1,2:T(8,128)S(1)}, f32[8,2,64,128]{3,0,1,2:T(8,128)S(1)}) fusion(f32[]{:T(128)} %bitcast.452, f32[]{:T(128)} %bitcast.448, f32[]{:T(128)} %bitcast.447, f32[]{:T(128)} %bitcast.446, f32[]{:T(128)} %bitcast.445, f32[]{:T(128)} %bitcast.444, bf16[64,8,2,1,128]{4,1,3,2,0:T(8,128)(2,1)S(1)} %all-to-all-done, ...), kind=kLoop, calls=%fused_computation.884 | loop fusion | flops 2752512 | bytes 2375724 | tf_op jit(solution)/shard_map/mul | solution.py:27
  609.9 105.8 %fusion.609 = bf16[8,2,64,128]{3,0,1,2:T(8,128)(2,1)S(1)} fusion(f32[8,2,66,128]{3,0,1,2:T(8,128)S(1)} %pad.206, f32[8,2,64,128]{3,0,1,2:T(8,128)S(1)} %fusion.608, f32[]{:T(128)} %bitcast.741, f32[]{:T(128)} %bitcast.740, f32[]{:T(128)} %bitcast.739, f32[]{:T(128)} %bitcast.738, f32[]{:T(128)} %bitcast.737, f32[]{:T(128)} %bitcast.736, f32[]{:T(128)} %bitcast.735, ...), kind=kLoop, calls=%fused_computation.881 | loop fusion | flops 37748736 | bytes 34079292 | tf_op jit(solution)/shard_map/convert_element_type | solution.py:110
  (154 shorter events, 255.1 us)
Async XLA Ops:
  6.5 115.4 %copy-start = (bf16[1,128,1024]{2,1,0:T(8,128)(2,1)S(1)}, bf16[1,128,1024]{2,1,0:T(8,128)(2,1)}, u32[]{:S(2)}) copy-start(bf16[1,128,1024]{2,1,0:T(8,128)(2,1)} %param.8) | copy-start | bytes 786436
  6.5 112.7 %all-gather.2.cloned.1.call-start = ((), (), s32[]{:S(2)}) async-start(), calls=%async_computation.1 | async-start | bytes 2129920 | tf_op jit(solution)/shard_map/all_gather | solution.py:65
  122.8 7.9 %collective-permute-start.1 = (bf16[2,128,1,128]{3,0,1,2:T(2,128)(2,1)S(1)}, bf16[2,128,1,128]{3,0,1,2:T(2,128)(2,1)S(1)}, u32[]{:S(2)}, u32[]{:S(2)}) collective-permute-start(bf16[2,128,1,128]{3,0,1,2:T(2,128)(2,1)S(1)} %copy.208), channel_id=1, source_target_pairs={{1,0},{2,1},{3,2},{5,4},{6,5},{7,6},{9,8},{10,9},{11,10},{13,12},{... | collective-permute-start | bytes 196616 | tf_op jit(solution)/shard_map/ppermute | solution.py:15
  124.2 6.6 collective-permute-start
  138.3 3.0 copy-start.1
  261.4 223.1 %copy-start.2 = (f32[16,9]{1,0:T(8,128)S(1)}, f32[16,9]{1,0:T(8,128)}, u32[]{:S(2)}) copy-start(f32[16,9]{1,0:T(8,128)} %param.15) | copy-start | bytes 1732
  261.4 223.8 %copy-start.3 = (f32[16,9]{1,0:T(8,128)S(1)}, f32[16,9]{1,0:T(8,128)}, u32[]{:S(2)}) copy-start(f32[16,9]{1,0:T(8,128)} %param.13) | copy-start | bytes 1732
  476.4 17.6 %all-to-all-start = ((bf16[64,8,2,1,128]{4,1,3,2,0:T(8,128)(2,1)}), bf16[64,8,2,1,128]{4,1,3,2,0:T(8,128)(2,1)S(1)}, u32[]{:S(2)}, u32[]{:S(2)}) async-start(bf16[64,8,2,1,128]{4,1,3,2,0:T(8,128)(2,1)} %constant_dynamic-update-slice_fusion), calls=%async_computation | async-start | bytes 524288 | tf_op jit(solution)/shard_map/all_to_all | solution.py:99
Sparse Core Ops, SparseCore 0:
  9.2 109.9 all-gather.1
